TPU v7x, 512 devices: a whole 4x8x8 slice. The times are simulated.
512 devices in a mesh: rep: 32 (over x_lo, y, core), fsdp: 16 (over z, x_hi).
Axes of the slice: x: 4 (x_hi: 2, x_lo: 2; x = x_hi * 2 + x_lo), y: 8, z: 8, core: 2. Of those that a mesh axis runs over, the one named last changes fastest.
Arguments:
- inputs: bfloat16 [32, 4096, 4096], P('rep', 'fsdp'), may hold values from -6 to 6
- up_grads: bfloat16 [32, 4096, 512], P('rep', 'fsdp'), may hold values from -0.09375 to 0.09375
- momentum: float32 [32, 4096, 512], P('rep', 'fsdp'), may hold values from -6 to 6
- selected: int32 [32, 64, 8, 32], P('rep', 'fsdp'), may hold values from 0 to 4095, as said below
Outputs:
- new_momentum: float32 [32, 4096, 512], P('rep', 'fsdp')
- update: bfloat16 [4096, 512], P('fsdp')
Inputs may be any that keep to these rules, and one draw needn't show every extreme that they name: `selected`: each list holds 32 different row-major positions of a 64 x 64 block, chosen by each replica on its own (for example from earlier magnitudes), so other replicas cannot derive them; they differ between replicas and blocks.
All inputs are finite; a program needn't handle non-finite values.
Results may differ from a plain program's by a relative error of at most 0.017.
Values may be sent and summed in bfloat16 or wider, within the bound.
A program may use at most 128 MiB of HBM per device.

v0:
```python
import jax
import jax.numpy as jnp
from jax import lax
from jax.sharding import PartitionSpec as P

SPAN = 64


highest = lax.Precision.HIGHEST
momentum_decay = 0.999
epsilon = 1e-06


def cosine_basis():
    freq = jnp.arange(SPAN, dtype=jnp.float32)[:, None]
    sample = jnp.arange(SPAN, dtype=jnp.float32)[None, :]
    cosines = jnp.cos(jnp.pi * (2.0 * sample + 1.0) * freq / (2.0 * SPAN))
    factor = jnp.where(freq == 0, jnp.sqrt(1.0 / SPAN), jnp.sqrt(2.0 / SPAN))
    return cosines * factor


def split_spans(field):
    return field.reshape(field.shape[0] // SPAN, SPAN, field.shape[1] // SPAN, SPAN).transpose(
        0, 2, 1, 3
    )


def join_spans(blocks):
    return blocks.transpose(0, 2, 1, 3).reshape(blocks.shape[0] * SPAN, blocks.shape[1] * SPAN)


def forward_cosine(blocks, cosines):
    partly = jnp.einsum("ui,rcij->rcuj", cosines, blocks, precision=highest)
    return jnp.einsum("rcuj,vj->rcuv", partly, cosines, precision=highest)


def basis_rows(indices, cosines):
    lane_ids = jnp.arange(SPAN, dtype=jnp.int32)
    hot_left = (indices[..., None] // SPAN == lane_ids).astype(jnp.float32)
    hot_right = (indices[..., None] % SPAN == lane_ids).astype(jnp.float32)
    rows_left = jnp.einsum("...kn,nj->...kj", hot_left, cosines, precision=highest)
    rows_right = jnp.einsum("...kn,nj->...kj", hot_right, cosines, precision=highest)
    return (rows_left, rows_right)


def decode_replicas(values, indices, cosines):
    rows_left, rows_right = basis_rows(indices, cosines)
    weighted = rows_left * values[..., None]
    return jnp.einsum("rabki,rabkj->abij", weighted, rows_right, precision=highest)


def local(inputs, up_grads, momentum, selected):
    tokens = inputs[0]
    signals = up_grads[0]
    moment = momentum[0]
    chosen = selected[0]
    gradient = lax.psum_scatter(
        lax.dot_general(
            tokens, signals, (((0,), (0,)), ((), ())), preferred_element_type=jnp.float32
        ).astype(jnp.bfloat16),
        "fsdp",
        scatter_dimension=0,
        tiled=True,
    ).astype(jnp.float32)
    stepped = momentum_decay * moment + gradient
    blocks = split_spans(stepped)
    cosines = cosine_basis()
    rows_left, rows_right = basis_rows(chosen, cosines)
    coefs = forward_cosine(blocks, cosines)
    picked = jnp.take_along_axis(
        coefs.reshape(blocks.shape[0], blocks.shape[1], SPAN * SPAN), chosen, axis=2
    )
    own_part = jnp.einsum(
        "abki,abkj->abij", rows_left * picked[..., None], rows_right, precision=highest
    )
    new_moment = stepped - join_spans(own_part)
    values, indices = (
        lax.all_gather(picked[None], "rep", axis=0, tiled=True),
        lax.all_gather(chosen[None], "rep", axis=0, tiled=True),
    )
    decoded = decode_replicas(values, indices, cosines)
    magnitude = jnp.sqrt(jnp.mean(decoded * decoded, axis=(2, 3), keepdims=True) + epsilon)
    update = join_spans(decoded / magnitude).astype(jnp.bfloat16)
    return (new_moment[None], update)


def solution(mesh):
    placed = (
        P("rep", "fsdp", None),
        P("rep", "fsdp", None),
        P("rep", "fsdp", None),
        P("rep", "fsdp", None, None),
    )
    return jax.shard_map(
        local,
        mesh=mesh,
        in_specs=placed,
        out_specs=(P("rep", "fsdp", None), P("fsdp", None)),
        check_vma=False,
    )
```

profile of v0, /device:TPU:1, one launch (start us, length us, event | category | flops | bytes accessed | tf_op | source)
XLA Modules:
  0.0 346.4 jit_solution(8930144033947326734)
XLA Ops:
  7.2 1.5 copy-done
  8.8 4.3 %convolution_convert_fusion = bf16[4096,512]{1,0:T(8,128)(2,1)} fusion(bf16[1,256,4096]{2,1,0:T(8,128)(2,1)S(1)} %copy-done, bf16[1,256,512]{2,1,0:T(8,128)(2,1)} %param.5), kind=kOutput, calls=%fused_computation.10 | convolution fusion | flops 1075838976 | bytes 6553600 | tf_op jit(solution)/shard_map/dot_general | solution.py:58
  13.1 0.7 fusion.28
  13.8 0.1 reshape.206
  13.9 38.9 %all_gather.6 = s32[32,4,8,32]{3,2,1,0:T(8,128)S(1)} all-gather(s32[1,4,8,32]{3,2,1,0:T(8,128)} %param.7), channel_id=1, replica_groups=mesh['rep'=32,'fsdp'=16] {'rep'}, dimensions={0}, use_global_device_ids=true | all-gather | bytes 135168 | tf_op jit(solution)/shard_map/all_gather | solution.py:79
  52.8 1.2 add_select_fusion.1
  54.0 0.3 copy.14
  54.3 1.3 copy.16
  55.7 1.3 fusion.13
  57.0 11.8 %fusion.3 = f32[32,4,8,32,64]{4,0,3,2,1:T(8,128)} fusion(s32[32,4,8,32]{0,3,2,1:T(8,128)S(1)} %copy.16, f32[64]{0:T(128)S(1)} %get-tuple-element.8, f32[64]{0:T(128)S(1)} %get-tuple-element.9), kind=kOutput, calls=%fused_computation.6 | convolution fusion | flops 1612722176 | bytes 8520192 | tf_op jit(solution)/shard_map/...kn,nj->...kj/dot_general | solution.py:42
  68.8 11.8 %fusion.2 = f32[32,4,8,32,64]{4,0,3,2,1:T(8,128)} fusion(s32[32,4,8,32]{0,3,2,1:T(8,128)S(1)} %copy.14, f32[64]{0:T(128)S(1)} %get-tuple-element.8, f32[64]{0:T(128)S(1)} %get-tuple-element.9), kind=kOutput, calls=%fused_computation.5 | convolution fusion | flops 1612722176 | bytes 8520192 | tf_op jit(solution)/shard_map/...kn,nj->...kj/dot_general | solution.py:41
  80.5 151.9 %reduce-scatter.2.cloned.1.call-done = bf16[256,512]{1,0:T(8,128)(2,1)} async-done(((bf16[4096,512]{1,0:T(8,128)(2,1)}), bf16[256,512]{1,0:T(8,128)(2,1)}) %reduce-scatter.2.cloned.1.call-update) | async-done | bytes 262160 | tf_op jit(solution)/shard_map/reduce_scatter | solution.py:57
  232.4 1.0 bitcast_add_fusion
  233.5 1.2 reshape.203
  234.7 2.6 copy.11
  237.3 2.3 convolution_bitcast_fusion.1
  239.6 2.8 fusion.22
  242.4 1.6 reshape.204
  244.0 8.6 %gather_fusion = f32[1024]{0:T(1024)S(1)} fusion(f32[4,8,4096]{2,1,0:T(8,128)S(1)} %reshape.204, s32[1024]{0:T(1024)S(1)} %reshape.206), kind=kCustom, calls=%fused_computation | custom fusion | bytes 20480 | tf_op jit(solution)/shard_map/jit(take_along_axis)/gather | solution.py:70
  252.5 0.1 gather.7
  252.6 0.1 reshape.209
  252.7 0.5 convolution_multiply_fusion
  253.2 3.0 convolution_bitcast_fusion
  256.2 1.6 copy.13
  257.8 1.5 reshape.205
  259.3 0.9 subtract_bitcast_fusion
  260.2 39.5 %all_gather.7 = f32[32,4,8,32]{3,2,1,0:T(8,128)S(1)} all-gather(f32[1,4,8,32]{3,2,1,0:T(8,128)S(1)} %and_select_fusion), channel_id=1, replica_groups=mesh['rep'=32,'fsdp'=16] {'rep'}, dimensions={0}, use_global_device_ids=true | all-gather | bytes 135168 | tf_op jit(solution)/shard_map/all_gather | solution.py:78
  299.7 1.1 copy.15
  300.8 37.1 %multiply_reduce_fusion = (f32[4,8]{1,0:T(4,128)S(1)}, f32[4,8,64,64]{3,2,1,0:T(8,128)S(1)}) fusion(f32[32,4,8,32,64]{4,0,3,2,1:T(8,128)} %fusion.3, f32[32,4,8,32,64]{4,0,3,2,1:T(8,128)} %fusion.2, f32[32,4,8,32]{0,3,2,1:T(8,128)} %copy.15), kind=kOutput, calls=%fused_computation.18 | convolution fusion | flops 1612972032 | bytes 17432704 | tf_op jit(solution)/shard_map/rabki,rabkj->abij/dot_general | solution.py:49
  337.9 0.2 fusion.12
  338.1 0.3 copy.17
  338.5 1.0 convert_element_type.23
  (12 shorter events, 0.1 us)
Async XLA Ops:
  7.2 1.6 copy-start
  7.2 48.5 %copy-start.2 = (s32[1,4,8,32]{3,2,1,0:T(8,128)S(1)}, s32[1,4,8,32]{3,2,1,0:T(8,128)}, u32[]{:S(2)}) copy-start(s32[1,4,8,32]{3,2,1,0:T(8,128)} %param.7) | copy-start | bytes 12292
  7.2 225.3 %reduce-scatter.2.cloned.1.call-start = ((), (), s32[]{:S(2)}) async-start(), calls=%async_computation.1 | async-start | bytes 4456448 | tf_op jit(solution)/shard_map/reduce_scatter | solution.py:57
  68.8 163.7 %copy-start.1 = (f32[1,256,512]{2,1,0:T(8,128)S(1)}, f32[1,256,512]{2,1,0:T(8,128)}, u32[]{:S(2)}) copy-start(f32[1,256,512]{2,1,0:T(8,128)} %param.6) | copy-start | bytes 1572868
Sparse Core Ops, SparseCore 0:
  13.2 219.1 reduce-scatter.1
where the time goes:
time: 347 us; the launch traced here: 346 us
  waiting for transfers between devices  152 us (44%)
  blocking collectives  78.4 us (23%)
  matrix products  74.9 us (22%)
  local copies, waits for them, and re-layouts  22.9 us (7%)
  between operations  14.1 us (4%)
  other arithmetic  4.1 us (1%)
    reduce_scatter x1, waiting for transfers between devices, local(): lax.psum_scatter(lax.dot_general(tokens, signals, (((0,), (0,)), ((), ())...  152 us
    all_gather x1, blocking collectives, local(): lax.all_gather(picked[None], 'rep', axis=0, tiled=True)  39.5 us
    all_gather x1, blocking collectives, local(): lax.all_gather(chosen[None], 'rep', axis=0, tiled=True)  38.9 us
    dot_general x1, matrix products, decode_replicas(): jnp.einsum('rabki,rabkj->abij', weighted, rows_right, precision=highest)  37.1 us
    dot_general x2, matrix products, basis_rows(): jnp.einsum('...kn,nj->...kj', hot_right, cosines, precision=highest)  13.1 us
    dot_general x2, matrix products, basis_rows(): jnp.einsum('...kn,nj->...kj', hot_left, cosines, precision=highest)  12.3 us
    gather x4, local copies, waits for them, and re-layouts, local(): jnp.take_along_axis(coefs.reshape(blocks.shape[0], blocks.shape[1], SPAN...  8.78 us
  transfers between devices with their start and end apart: 1, of which 1 were waited for; matrix products, arithmetic and copies ran while one was open for 8% of the time, Pallas kernels for 0%

commit v1 on v0

v1 whole, which is shorter than its diff:
```python
import jax
import jax.numpy as jnp
import numpy as np
from jax import lax
from jax.experimental import pallas as pl
from jax.experimental.pallas import tpu as pltpu
from jax.sharding import PartitionSpec as P

MESH = pl.DeviceIdType.MESH
F32, BF16 = jnp.float32, jnp.bfloat16
SPAN, ROWS, COLS, TOK, RING, REPS = 64, 256, 512, 256, 8, 32
HALF = COLS // 2
LISTS = 8
decay, epsilon = 0.999, 1e-06
FIRST = 3
STREAMS = 5
STREAM_ROWS = 32 + 3 * SPAN


def split(x):
    hi = x.astype(BF16)
    return hi, (x - hi.astype(F32)).astype(BF16)


def constants():
    freq = np.arange(SPAN, dtype=np.float64)[:, None]
    sample = np.arange(SPAN, dtype=np.float64)[None, :]
    basis = np.cos(np.pi * (2.0 * sample + 1.0) * freq / (2.0 * SPAN))
    basis = basis * np.where(freq == 0, np.sqrt(1.0 / SPAN), np.sqrt(2.0 / SPAN))
    hi = basis.astype(BF16)
    lo = (basis - hi.astype(np.float64)).astype(BF16)

    def left(a, b):
        return np.concatenate([a, a, b, b], axis=1)

    def right(a):
        return np.kron(np.eye(4), a.astype(np.float64)).astype(BF16)

    lefts = np.stack([left(hi, lo), left(hi.T, lo.T)])
    rights = np.stack([right(hi.T), right(lo.T), right(hi), right(lo), right(np.ones((SPAN, SPAN)))])
    return lefts, rights


def dot(a, b):
    return jnp.dot(a, b, preferred_element_type=F32)


def dot_lanes(a, b):
    return lax.dot_general(a, b, (((1,), (1,)), ((), ())), preferred_element_type=F32)


def from_left(const, x):
    hi, lo = split(x)
    return dot(const, jnp.concatenate([hi, lo, hi, lo], axis=0))


def from_right(x, const_hi, const_lo):
    hi, lo = split(x)
    both = dot(jnp.concatenate([hi, lo], axis=0), const_hi)
    return both[: x.shape[0]] + both[x.shape[0] :] + dot(hi, const_lo)


def offset(way, stream, step):
    return (way * STREAMS + stream) * STREAM_ROWS + (0 if step == 0 else 32 + SPAN * (step - 1))


def kernel(
    x_hbm, g_hbm, m_hbm, sel_ref, left_ref, right_ref, new_hbm, upd_hbm,
    x_in, xt, x_got, g_own, g_got, mom, sums_out, sums_in, b_out, b_in, part, grad, coef, mask,
    ids, vals, l_hot, r_hot, r_own, new_v, upd_v,
    load_sem, xs_sem, xr_sem, zs_sem, zr_sem, is_sem, ir_sem, vs_sem, vr_sem, out_sem,
):
    rep, fsdp = lax.axis_index("rep"), lax.axis_index("fsdp")
    core, y, x_lo = rep % 2, (rep // 2) % 8, rep // 16
    z, x_hi = fsdp // 2, fsdp % 2
    partner = (rep, z * 2 + 1 - x_hi)
    ways = [(rep, ((z + 1) % RING) * 2 + x_hi), (rep, ((z + RING - 1) % RING) * 2 + x_hi)]
    peers = [
        (((x_lo + dx) % 2) * 16 + ((y + dy) % 8) * 2 + (core + dc) % 2, fsdp)
        for dy in (4, 3, 5, 2, 6, 1, 7, 0)
        for dx in (0, 1)
        for dc in (0, 1)
        if (dy, dx, dc) != (0, 0, 0)
    ]

    g_load = pltpu.make_async_copy(g_hbm.at[0], g_own, load_sem.at[0])
    g_load.start()
    order = (4, 3, 5, 2, 6, 1, 7, 0)
    x_loads = {}
    for n, dz in enumerate(order):
        for kind in (1, 0):
            column = ((z + dz) % RING) * 512 + (x_hi if kind == 0 else 1 - x_hi) * 256
            cp = pltpu.make_async_copy(
                x_hbm.at[0, :, pl.ds(pl.multiple_of(column, 256), 256)],
                x_in.at[dz, kind],
                load_sem.at[2 + 2 * n + kind],
            )
            cp.start()
            x_loads[dz, kind] = cp
    m_load = pltpu.make_async_copy(m_hbm.at[0], mom, load_sem.at[1])
    m_load.start()

    barrier = pltpu.get_barrier_semaphore()
    for device in [partner, *ways, *peers]:
        pl.semaphore_signal(barrier, inc=1, device_id=device, device_id_type=MESH)

    rows = []
    for a in range(4):
        for h in range(2):
            rows.append(jnp.concatenate([sel_ref[0, a, 4 * h + j : 4 * h + j + 1, :] for j in range(4)], axis=1))
    own_ids = jnp.concatenate(rows, axis=0)
    ids[pl.ds(rep, 1)] = own_ids[None]

    pl.semaphore_wait(barrier, 3 + len(peers))

    g_load.wait()

    def remote(src, dst, send_sem, recv_sem, device):
        cp = pltpu.make_async_remote_copy(
            src_ref=src, dst_ref=dst, send_sem=send_sem, recv_sem=recv_sem, device_id=device, device_id_type=MESH
        )
        cp.start()
        return cp

    x_sends = [remote(g_own, g_got, xs_sem.at[8], xr_sem.at[8], partner)]
    id_sends = [
        remote(ids.at[pl.ds(rep, 1)], ids.at[pl.ds(rep, 1)], is_sem.at[0], ir_sem.at[0], device) for device in peers
    ]
    for dz in order:
        for kind in (1, 0):
            x_loads[dz, kind].wait()
            xt[dz, kind] = x_in[dz, kind].T
        x_sends.append(
            remote(
                xt.at[dz, 1, pl.ds(0, FIRST * SPAN)], x_got.at[dz], xs_sem.at[dz], xr_sem.at[dz], partner
            )
        )

    def wait_x(dz):
        x_sends[1 + order.index(dz)].wait_recv()

    def product(stream, dz):
        if stream < FIRST:
            at = pl.ds(stream * SPAN, SPAN)
            return dot(xt[dz, 0, at], g_own[...]) + dot(x_got[dz, at], g_got[...])
        return dot(xt[dz, 0 if stream == 3 else 1, pl.ds(FIRST * SPAN, SPAN)], g_own[...])

    z_copies = {}

    def send_sum(way, stream, step):
        size = 32 if step == 0 else SPAN
        at = pl.ds(offset(way, stream, step), size)
        z_copies[way, stream, step] = remote(
            sums_out.at[at], sums_in.at[at], zs_sem.at[0], zr_sem.at[way, stream, step], ways[way]
        )

    def arrived(way, stream, step):
        z_copies[way, stream, step].wait_recv()
        size = 32 if step == 0 else SPAN
        return sums_in[pl.ds(offset(way, stream, step), size), :].astype(F32)

    def chain(stream, step):
        if step == 0:
            term = product(stream, 4).astype(BF16)
            for way in range(2):
                sums_out[pl.ds(offset(way, stream, 0), 32), :] = term[32 * way : 32 * way + 32]
                send_sum(way, stream, 0)
            return
        for way in range(2):
            term = product(stream, 4 - step if way == 0 else 4 + step)
            got = arrived(way, stream, step - 1)
            at = offset(way, stream, step)
            if step == 1:
                for part_ in range(2):
                    piece = term[32 * part_ : 32 * part_ + 32]
                    piece = piece + got if part_ == way else piece
                    sums_out[pl.ds(at + 32 * part_, 32), :] = piece.astype(BF16)
            else:
                sums_out[pl.ds(at, SPAN), :] = (term + got).astype(BF16)
            send_sum(way, stream, step)

    def finish(stream):
        return product(stream, 0) + arrived(0, stream, 3) + arrived(1, stream, 3)

    lane = lax.broadcasted_iota(jnp.int32, (1, 128), 1)
    count_u = lax.broadcasted_iota(jnp.int32, (SPAN, 128), 0)
    count_n = lax.broadcasted_iota(jnp.int32, (HALF, 128), 0)

    def hot(row):
        by_row = (row >> 6) == count_u
        by_column = (row & 63) + (lane >> 5) * SPAN == count_n
        return by_row.astype(F32).astype(BF16), by_column.astype(F32).astype(BF16)

    def build(first, count):
        def one(r, carry):
            at = pl.ds(pl.multiple_of(r * 128, 128), 128)
            for s in range(LISTS):
                l, n = hot(ids[r, s : s + 1, :])
                l_hot[s, :, at] = l
                r_hot[s, :, at] = n
            return carry

        lax.fori_loop(first, first + count, one, 0)

    def own_mask():
        for s in range(LISTS):
            l, n = hot(own_ids[s : s + 1])
            r_own[s] = n
            a, h = s // 2, s % 2
            mask[pl.ds(a * SPAN, SPAN), pl.ds(h * HALF, HALF)] = dot_lanes(l, n)

    def transform(a):
        at = pl.ds(a * SPAN, SPAN)
        stepped = decay * mom[at, :] + grad[at, :]
        grad[at, :] = stepped
        partly = from_left(left_ref[0], stepped)
        kept = []
        for h in range(2):
            c = from_right(partly[:, h * HALF : (h + 1) * HALF], right_ref[0], right_ref[1])
            coef[at, pl.ds(h * HALF, HALF)] = c
            s = 2 * a + h
            hi, lo = split(c)
            both = dot(jnp.concatenate([hi, lo], axis=0), r_own[s])
            by_row = (own_ids[s : s + 1] >> 6) == count_u
            kept.append(jnp.sum(jnp.where(by_row, both[:SPAN] + both[SPAN:], 0.0), axis=0, keepdims=True))
        vals[pl.ds(rep, 1), pl.ds(2 * a, 2)] = jnp.concatenate(kept, axis=0)[None]

    chain(3, 0)
    chain(4, 0)
    own_mask()
    chain(3, 1)
    chain(4, 1)
    chain(3, 2)
    chain(4, 2)
    x_sends[0].wait_recv()
    wait_x(4)
    for s in range(FIRST):
        chain(s, 0)
    chain(4, 3)
    chain(3, 3)
    most = pltpu.make_async_remote_copy(
        src_ref=ids.at[pl.ds(0, REPS - 1)], dst_ref=ids.at[pl.ds(0, REPS - 1)],
        send_sem=is_sem.at[0], recv_sem=ir_sem.at[0], device_id=partner, device_id_type=MESH,
    )
    most.wait_recv()
    build(0, 8)
    wait_x(3)
    wait_x(5)
    for s in range(FIRST):
        chain(s, 1)
    build(8, 8)
    wait_x(2)
    wait_x(6)
    for s in range(FIRST):
        chain(s, 2)
    b_out[...] = finish(4).astype(BF16)
    b_send = remote(b_out, b_in, xs_sem.at[9], xr_sem.at[9], partner)
    build(16, 8)
    wait_x(1)
    wait_x(7)
    for s in range(FIRST):
        chain(s, 3)
    build(24, 8)
    m_load.wait()
    own = finish(3)
    b_send.wait_recv()
    grad[pl.ds(FIRST * SPAN, SPAN), :] = own + b_in[...].astype(F32)
    transform(3)
    wait_x(0)
    for s in range(FIRST):
        grad[pl.ds(s * SPAN, SPAN), :] = finish(s)
        transform(s)

    val_sends = [
        remote(vals.at[pl.ds(rep, 1)], vals.at[pl.ds(rep, 1)], vs_sem.at[0], vr_sem.at[0], device) for device in peers
    ]
    for a in range(4):
        at = pl.ds(a * SPAN, SPAN)
        partly = from_left(left_ref[1], coef[at, :] * mask[at, :])
        for h in range(2):
            cols = pl.ds(h * HALF, HALF)
            own = from_right(partly[:, h * HALF : (h + 1) * HALF], right_ref[2], right_ref[3])
            new_v[at, cols] = grad[at, cols] - own
    new_store = pltpu.make_async_copy(new_v, new_hbm.at[0], out_sem.at[0])
    new_store.start()

    most_vals = pltpu.make_async_remote_copy(
        src_ref=vals.at[pl.ds(0, REPS - 1)], dst_ref=vals.at[pl.ds(0, REPS - 1)],
        send_sem=vs_sem.at[0], recv_sem=vr_sem.at[0], device_id=partner, device_id_type=MESH,
    )
    most_vals.wait_recv()
    total = []
    for s in range(LISTS):
        weighted = jnp.concatenate(
            [l_hot[s, :, r * 128 : (r + 1) * 128] * vals[r, s : s + 1, :].astype(BF16) for r in range(REPS)], axis=1
        )
        total.append(dot_lanes(weighted, r_hot[s]))
    power = jnp.concatenate([jnp.sum(t * t, axis=0, keepdims=True) for t in total], axis=0)
    hi, lo = split(power)
    power = dot(hi, right_ref[4]) + dot(lo, right_ref[4])
    scale = lax.rsqrt(power * (1.0 / (SPAN * SPAN)) + epsilon)
    for s in range(LISTS):
        decoded = from_right(from_left(left_ref[1], total[s]), right_ref[2], right_ref[3])
        at = (pl.ds((s // 2) * SPAN, SPAN), pl.ds((s % 2) * HALF, HALF))
        upd_v[at] = (decoded * scale[s : s + 1]).astype(BF16)
    upd_store = pltpu.make_async_copy(upd_v, upd_hbm, out_sem.at[1])
    upd_store.start()

    for cp in x_sends:
        cp.wait_send()
    b_send.wait_send()
    pltpu.make_async_remote_copy(
        src_ref=sums_out, dst_ref=sums_out, send_sem=zs_sem.at[0], recv_sem=zr_sem.at[0, 0, 0],
        device_id=partner, device_id_type=MESH,
    ).wait_send()
    most.wait_send()
    most_vals.wait_send()
    new_store.wait()
    upd_store.wait()


def local(inputs, up_grads, momentum, selected):
    lefts, rights = constants()
    vmem, hbm = pl.BlockSpec(memory_space=pltpu.VMEM), pl.BlockSpec(memory_space=pl.ANY)
    sums = STREAMS * 2 * STREAM_ROWS
    return pl.pallas_call(
        kernel,
        out_shape=(
            jax.ShapeDtypeStruct((1, ROWS, COLS), F32),
            jax.ShapeDtypeStruct((ROWS, COLS), BF16),
        ),
        in_specs=[hbm, hbm, hbm, vmem, vmem, vmem],
        out_specs=(hbm, hbm),
        scratch_shapes=[
            pltpu.VMEM((RING, 2, TOK, ROWS), BF16),
            pltpu.VMEM((RING, 2, ROWS, TOK), BF16),
            pltpu.VMEM((RING, FIRST * SPAN, TOK), BF16),
            pltpu.VMEM((TOK, COLS), BF16),
            pltpu.VMEM((TOK, COLS), BF16),
            pltpu.VMEM((ROWS, COLS), F32),
            pltpu.VMEM((sums, COLS), BF16),
            pltpu.VMEM((sums, COLS), BF16),
            pltpu.VMEM((SPAN, COLS), BF16),
            pltpu.VMEM((SPAN, COLS), BF16),
            pltpu.VMEM((SPAN, COLS), F32),
            pltpu.VMEM((ROWS, COLS), F32),
            pltpu.VMEM((ROWS, COLS), F32),
            pltpu.VMEM((ROWS, COLS), F32),
            pltpu.VMEM((REPS, LISTS, 128), jnp.int32),
            pltpu.VMEM((REPS, LISTS, 128), F32),
            pltpu.VMEM((LISTS, SPAN, REPS * 128), BF16),
            pltpu.VMEM((LISTS, HALF, REPS * 128), BF16),
            pltpu.VMEM((LISTS, HALF, 128), BF16),
            pltpu.VMEM((ROWS, COLS), F32),
            pltpu.VMEM((ROWS, COLS), BF16),
            pltpu.SemaphoreType.DMA((18,)),
            pltpu.SemaphoreType.DMA((10,)),
            pltpu.SemaphoreType.DMA((10,)),
            pltpu.SemaphoreType.DMA((1,)),
            pltpu.SemaphoreType.DMA((2, STREAMS, 4)),
            pltpu.SemaphoreType.DMA((1,)),
            pltpu.SemaphoreType.DMA((1,)),
            pltpu.SemaphoreType.DMA((1,)),
            pltpu.SemaphoreType.DMA((1,)),
            pltpu.SemaphoreType.DMA((2,)),
        ],
        compiler_params=pltpu.CompilerParams(
            collective_id=0, has_side_effects=True, vmem_limit_bytes=56 * 1024 * 1024
        ),
        cost_estimate=pl.CostEstimate(flops=4 * 10**9, bytes_accessed=8 * 10**6, transcendentals=0),
    )(inputs, up_grads, momentum, selected, jnp.asarray(lefts), jnp.asarray(rights))


def solution(mesh):
    placed = (
        P("rep", "fsdp", None),
        P("rep", "fsdp", None),
        P("rep", "fsdp", None),
        P("rep", "fsdp", None, None),
    )
    return jax.shard_map(
        local,
        mesh=mesh,
        in_specs=placed,
        out_specs=(P("rep", "fsdp", None), P("fsdp", None)),
        check_vma=False,
    )
```

time: 347 us -> 66.7 us (0.19)
  waiting for transfers between devices: 152 us -> 0 us
  blocking collectives: 78.4 us -> 0 us
  matrix products: 74.9 us -> 0 us
  Pallas kernels: 0 us -> 62.3 us
  local copies, waits for them, and re-layouts: 22.9 us -> 3.54 us
  between operations: 14.1 us -> 0.64 us
  other arithmetic: 4.1 us -> 0 us
    reduce_scatter x1 -> x0, waiting for transfers between devices: 152 us -> none  [local(): lax.psum_scatter(lax.dot_general(tokens, signals, (((0,), (0,)), ((), ())...]
    all_gather x2 -> x0, blocking collectives: 78.4 us -> none  [the longest x1 39.5 us: local(): lax.all_gather(picked[None], 'rep', axis=0, tiled=True)]
    dot_general x9 -> x0, matrix products: 74.9 us -> none  [the longest x1 37.1 us: decode_replicas(): jnp.einsum('rabki,rabkj->abij', weighted, rows_right, precision=highest)]
    pallas_call x0 -> x1, Pallas kernels: none -> 62.3 us  [local(): pl.pallas_call(kernel, out_shape=(jax.ShapeDtypeStruct((1, ROWS, COLS), F...]
    gather x4 -> x0, local copies, waits for them, and re-layouts: 8.78 us -> none  [local(): jnp.take_along_axis(coefs.reshape(blocks.shape[0], blocks.shape[1], SPAN...]
    reshape x4 -> x0, local copies, waits for them, and re-layouts: 6.84 us -> none  [the longest x2 3.77 us: split_spans(): field.reshape(field.shape[0] // SPAN, SPAN, field.shape[1] // SPAN, SPAN)]
  transfers between devices with their start and end apart: 1 -> 0, of which waited for: 1 -> 0; matrix products, arithmetic and copies ran while one was open for 8% -> 0% of each run, Pallas kernels for 0% -> 0%
where the time goes in v1:
time: 66.7 us; the launch traced here: 66.5 us
  Pallas kernels  62.3 us (93%)
  local copies, waits for them, and re-layouts  3.54 us (5%)
    pallas_call x1, Pallas kernels, local(): pl.pallas_call(kernel, out_shape=(jax.ShapeDtypeStruct((1, ROWS, COLS), F...  62.3 us
    unnamed x2, local copies, waits for them, and re-layouts  3.54 us

profile of v1, /device:TPU:1, one launch (start us, length us, event | category | flops | bytes accessed | tf_op | source)
XLA Modules:
  0.0 66.5 jit_solution(15502010964689341868)
XLA Ops:
  0.6 62.3 %shard_map.77 = (f32[1,256,512]{2,1,0:T(8,128)}, bf16[256,512]{1,0:T(8,128)(2,1)}) custom-call(bf16[1,256,4096]{2,1,0:T(8,128)(2,1)} %x_hbm.1, bf16[1,256,512]{2,1,0:T(8,128)(2,1)} %g_hbm.1, f32[1,256,512]{2,1,0:T(8,128)} %m_hbm.1, s32[1,4,8,32]{3,2,1,0:T(8,128)} %sel_ref.1, bf16[2,64,256]{2,1,0:T(8,128)(2,1)} %constant.4.clone.left_ref, ...), custom_call_target="tpu_custom_call" | custom-call | flops 4000000000 | bytes 8000000 | tf_op jit(solution)/shard_map/pallas_call | solution.py:326
  63.0 1.9 %copy.10 = f32[1,256,512]{2,1,0:T(8,128)} copy(f32[1,256,512]{2,1,0:T(8,128)} %get-tuple-element.4) | data formatting | bytes 1048576
  64.8 1.7 %copy.11 = bf16[256,512]{1,0:T(8,128)(2,1)} copy(bf16[256,512]{1,0:T(8,128)(2,1)} %get-tuple-element.5) | data formatting | bytes 524288

commit v2 on v1

--- a/solution.py
+++ b/solution.py
@@ -10,6 +10,7 @@
 F32, BF16 = jnp.float32, jnp.bfloat16
 SPAN, ROWS, COLS, TOK, RING, REPS = 64, 256, 512, 256, 8, 32
 HALF = COLS // 2
+AROUND = (0, 4, 3, 5, 2, 6, 1, 7)
 LISTS = 8
 decay, epsilon = 0.999, 1e-06
 FIRST = 3
@@ -65,9 +66,9 @@
 
 
 def kernel(
-    x_hbm, g_hbm, m_hbm, sel_ref, left_ref, right_ref, new_hbm, upd_hbm,
-    x_in, xt, x_got, g_own, g_got, mom, sums_out, sums_in, b_out, b_in, part, grad, coef, mask,
-    ids, vals, l_hot, r_hot, r_own, new_v, upd_v,
+    x_hbm, g_hbm, m_hbm, sel_hbm, left_hbm, right_hbm, new_hbm, upd_hbm,
+    sel_ref, left_ref, right_ref, x_in, xt, x_got, g_own, g_got, mom, sums_out, sums_in, b_out, b_in, grad, coef, mask,
+    ids, vals, l_hot, r_hot, r_own, total, new_v, upd_v,
     load_sem, xs_sem, xr_sem, zs_sem, zr_sem, is_sem, ir_sem, vs_sem, vr_sem, out_sem,
 ):
     rep, fsdp = lax.axis_index("rep"), lax.axis_index("fsdp")
@@ -75,14 +76,17 @@
     z, x_hi = fsdp // 2, fsdp % 2
     partner = (rep, z * 2 + 1 - x_hi)
     ways = [(rep, ((z + 1) % RING) * 2 + x_hi), (rep, ((z + RING - 1) % RING) * 2 + x_hi)]
-    peers = [
-        (((x_lo + dx) % 2) * 16 + ((y + dy) % 8) * 2 + (core + dc) % 2, fsdp)
-        for dy in (4, 3, 5, 2, 6, 1, 7, 0)
-        for dx in (0, 1)
-        for dc in (0, 1)
-        if (dy, dx, dc) != (0, 0, 0)
+    near = [
+        (((x_lo + dx) % 2) * 16 + y * 2 + (core + dc) % 2, fsdp) for dx in (0, 1) for dc in (0, 1) if dx + dc > 0
     ]
-
+    far = {dy: (x_lo * 16 + ((y + dy) % 8) * 2 + core, fsdp) for dy in AROUND[1:]}
+
+    barrier = pltpu.get_barrier_semaphore()
+    for device in [partner, *ways, *near, *far.values()]:
+        pl.semaphore_signal(barrier, inc=1, device_id=device, device_id_type=MESH)
+
+    sel_load = pltpu.make_async_copy(sel_hbm, sel_ref, load_sem.at[18])
+    sel_load.start()
     g_load = pltpu.make_async_copy(g_hbm.at[0], g_own, load_sem.at[0])
     g_load.start()
     order = (4, 3, 5, 2, 6, 1, 7, 0)
@@ -99,21 +103,20 @@
             x_loads[dz, kind] = cp
     m_load = pltpu.make_async_copy(m_hbm.at[0], mom, load_sem.at[1])
     m_load.start()
-
-    barrier = pltpu.get_barrier_semaphore()
-    for device in [partner, *ways, *peers]:
-        pl.semaphore_signal(barrier, inc=1, device_id=device, device_id_type=MESH)
-
+    left_load = pltpu.make_async_copy(left_hbm, left_ref, load_sem.at[19])
+    left_load.start()
+    right_load = pltpu.make_async_copy(right_hbm, right_ref, load_sem.at[20])
+    right_load.start()
+
+    sel_load.wait()
     rows = []
     for a in range(4):
         for h in range(2):
             rows.append(jnp.concatenate([sel_ref[0, a, 4 * h + j : 4 * h + j + 1, :] for j in range(4)], axis=1))
     own_ids = jnp.concatenate(rows, axis=0)
-    ids[pl.ds(rep, 1)] = own_ids[None]
-
-    pl.semaphore_wait(barrier, 3 + len(peers))
-
-    g_load.wait()
+    ids[0] = own_ids
+
+    pl.semaphore_wait(barrier, 3 + len(near) + len(far))
 
     def remote(src, dst, send_sem, recv_sem, device):
         cp = pltpu.make_async_remote_copy(
@@ -122,22 +125,20 @@
         cp.start()
         return cp
 
-    x_sends = [remote(g_own, g_got, xs_sem.at[8], xr_sem.at[8], partner)]
-    id_sends = [
-        remote(ids.at[pl.ds(rep, 1)], ids.at[pl.ds(rep, 1)], is_sem.at[0], ir_sem.at[0], device) for device in peers
-    ]
-    for dz in order:
-        for kind in (1, 0):
-            x_loads[dz, kind].wait()
-            xt[dz, kind] = x_in[dz, kind].T
-        x_sends.append(
-            remote(
-                xt.at[dz, 1, pl.ds(0, FIRST * SPAN)], x_got.at[dz], xs_sem.at[dz], xr_sem.at[dz], partner
-            )
-        )
+    x_sends = {}
+
+    def turn(*distances):
+        for dz in distances:
+            for kind in (1, 0):
+                x_loads[dz, kind].wait()
+                xt[dz, kind] = x_in[dz, kind].T
+                if kind == 1:
+                    x_sends[dz] = remote(
+                        xt.at[dz, 1, pl.ds(0, FIRST * SPAN)], x_got.at[dz], xs_sem.at[dz], xr_sem.at[dz], partner
+                    )
 
     def wait_x(dz):
-        x_sends[1 + order.index(dz)].wait_recv()
+        x_sends[dz].wait_recv()
 
     def product(stream, dz):
         if stream < FIRST:
@@ -191,13 +192,36 @@
         by_column = (row & 63) + (lane >> 5) * SPAN == count_n
         return by_row.astype(F32).astype(BF16), by_column.astype(F32).astype(BF16)
 
+    def send_near(slots, send_sem, recv_sem):
+        for n, device in enumerate(near):
+            remote(slots.at[0], slots.at[1 + n], send_sem.at[0], recv_sem.at[0], device)
+
+    def send_far(slots, send_sem, recv_sem):
+        landed(slots, recv_sem, 0)
+        for dy, device in far.items():
+            n = AROUND.index(8 - dy)
+            remote(slots.at[pl.ds(0, 4)], slots.at[pl.ds(4 * n, 4)], send_sem.at[1], recv_sem.at[n], device)
+
+    def of_size(slots, count, send_sem, recv_sem):
+        at = slots.at[pl.ds(0, count)]
+        return pltpu.make_async_remote_copy(
+            src_ref=at, dst_ref=at, send_sem=send_sem, recv_sem=recv_sem, device_id=partner, device_id_type=MESH
+        )
+
+    def landed(slots, recv_sem, n):
+        of_size(slots, 3 if n == 0 else 4, is_sem.at[0], recv_sem.at[n]).wait_recv()
+
+    def sent(slots, send_sem):
+        of_size(slots, 3, send_sem.at[0], ir_sem.at[0]).wait_send()
+        of_size(slots, 28, send_sem.at[1], ir_sem.at[0]).wait_send()
+
     def build(first, count):
         def one(r, carry):
             at = pl.ds(pl.multiple_of(r * 128, 128), 128)
             for s in range(LISTS):
                 l, n = hot(ids[r, s : s + 1, :])
                 l_hot[s, :, at] = l
-                r_hot[s, :, at] = n
+                r_hot[s, at, :] = n.T
             return carry
 
         lax.fori_loop(first, first + count, one, 0)
@@ -223,45 +247,57 @@
             both = dot(jnp.concatenate([hi, lo], axis=0), r_own[s])
             by_row = (own_ids[s : s + 1] >> 6) == count_u
             kept.append(jnp.sum(jnp.where(by_row, both[:SPAN] + both[SPAN:], 0.0), axis=0, keepdims=True))
-        vals[pl.ds(rep, 1), pl.ds(2 * a, 2)] = jnp.concatenate(kept, axis=0)[None]
-
+        vals[0, pl.ds(2 * a, 2)] = jnp.concatenate(kept, axis=0)
+
+    send_near(ids, is_sem, ir_sem)
+    g_send = remote(g_hbm.at[0], g_got, xs_sem.at[8], xr_sem.at[8], partner)
+    turn(4)
+    g_load.wait()
     chain(3, 0)
     chain(4, 0)
-    own_mask()
+    turn(3, 5)
+    send_far(ids, is_sem, ir_sem)
     chain(3, 1)
     chain(4, 1)
+    turn(2, 6)
     chain(3, 2)
     chain(4, 2)
-    x_sends[0].wait_recv()
+    turn(1, 7)
+    g_send.wait_recv()
     wait_x(4)
     for s in range(FIRST):
         chain(s, 0)
     chain(4, 3)
     chain(3, 3)
-    most = pltpu.make_async_remote_copy(
-        src_ref=ids.at[pl.ds(0, REPS - 1)], dst_ref=ids.at[pl.ds(0, REPS - 1)],
-        send_sem=is_sem.at[0], recv_sem=ir_sem.at[0], device_id=partner, device_id_type=MESH,
-    )
-    most.wait_recv()
-    build(0, 8)
+    turn(0)
+    own_mask()
+    build(0, 4)
     wait_x(3)
     wait_x(5)
-    for s in range(FIRST):
-        chain(s, 1)
-    build(8, 8)
+    chain(0, 1)
+    for n in range(1, 8):
+        landed(ids, ir_sem, n)
+    build(4, 3)
+    chain(1, 1)
+    build(7, 3)
+    chain(2, 1)
+    build(10, 2)
     wait_x(2)
     wait_x(6)
     for s in range(FIRST):
         chain(s, 2)
+        build(12 + 3 * s, 3)
     b_out[...] = finish(4).astype(BF16)
     b_send = remote(b_out, b_in, xs_sem.at[9], xr_sem.at[9], partner)
-    build(16, 8)
     wait_x(1)
     wait_x(7)
     for s in range(FIRST):
         chain(s, 3)
-    build(24, 8)
+        build(21 + 3 * s, 3)
+    build(30, 2)
     m_load.wait()
+    left_load.wait()
+    right_load.wait()
     own = finish(3)
     b_send.wait_recv()
     grad[pl.ds(FIRST * SPAN, SPAN), :] = own + b_in[...].astype(F32)
@@ -271,10 +307,10 @@
         grad[pl.ds(s * SPAN, SPAN), :] = finish(s)
         transform(s)
 
-    val_sends = [
-        remote(vals.at[pl.ds(rep, 1)], vals.at[pl.ds(rep, 1)], vs_sem.at[0], vr_sem.at[0], device) for device in peers
-    ]
+    send_near(vals, vs_sem, vr_sem)
     for a in range(4):
+        if a == 2:
+            send_far(vals, vs_sem, vr_sem)
         at = pl.ds(a * SPAN, SPAN)
         partly = from_left(left_ref[1], coef[at, :] * mask[at, :])
         for h in range(2):
@@ -284,18 +320,20 @@
     new_store = pltpu.make_async_copy(new_v, new_hbm.at[0], out_sem.at[0])
     new_store.start()
 
-    most_vals = pltpu.make_async_remote_copy(
-        src_ref=vals.at[pl.ds(0, REPS - 1)], dst_ref=vals.at[pl.ds(0, REPS - 1)],
-        send_sem=vs_sem.at[0], recv_sem=vr_sem.at[0], device_id=partner, device_id_type=MESH,
-    )
-    most_vals.wait_recv()
-    total = []
-    for s in range(LISTS):
-        weighted = jnp.concatenate(
-            [l_hot[s, :, r * 128 : (r + 1) * 128] * vals[r, s : s + 1, :].astype(BF16) for r in range(REPS)], axis=1
-        )
-        total.append(dot_lanes(weighted, r_hot[s]))
-    power = jnp.concatenate([jnp.sum(t * t, axis=0, keepdims=True) for t in total], axis=0)
+    for first, last in ((0, 1), (1, 4), (4, 6), (6, 8)):
+        for n in range(max(first, 1), last):
+            landed(vals, vr_sem, n)
+        for s in range(LISTS):
+            weighted = jnp.concatenate(
+                [
+                    l_hot[s, :, r * 128 : (r + 1) * 128] * vals[r, s : s + 1, :].astype(BF16)
+                    for r in range(4 * first, 4 * last)
+                ],
+                axis=1,
+            )
+            term = dot(weighted, r_hot[s, pl.ds(4 * first * 128, 4 * (last - first) * 128)])
+            total[s] = term if first == 0 else total[s] + term
+    power = jnp.concatenate([jnp.sum(total[s] * total[s], axis=0, keepdims=True) for s in range(LISTS)], axis=0)
     hi, lo = split(power)
     power = dot(hi, right_ref[4]) + dot(lo, right_ref[4])
     scale = lax.rsqrt(power * (1.0 / (SPAN * SPAN)) + epsilon)
@@ -306,32 +344,51 @@
     upd_store = pltpu.make_async_copy(upd_v, upd_hbm, out_sem.at[1])
     upd_store.start()
 
-    for cp in x_sends:
+    g_send.wait_send()
+    for cp in x_sends.values():
         cp.wait_send()
     b_send.wait_send()
     pltpu.make_async_remote_copy(
         src_ref=sums_out, dst_ref=sums_out, send_sem=zs_sem.at[0], recv_sem=zr_sem.at[0, 0, 0],
         device_id=partner, device_id_type=MESH,
     ).wait_send()
-    most.wait_send()
-    most_vals.wait_send()
+    sent(ids, is_sem)
+    sent(vals, vs_sem)
     new_store.wait()
     upd_store.wait()
 
 
+def hand_on(new_ref, upd_ref, new_out, upd_out, new_v, upd_v, load_sem, store_sem):
+    loads, stores = [], []
+    for n in range(8):
+        held, src, dst = (new_v, new_ref.at[0], new_out.at[0]) if n < 4 else (upd_v, upd_ref, upd_out)
+        at = pl.ds((n % 4) * SPAN, SPAN)
+        loads.append(pltpu.make_async_copy(src.at[at], held.at[at], load_sem.at[n]))
+        stores.append(pltpu.make_async_copy(held.at[at], dst.at[at], store_sem.at[n]))
+        loads[n].start()
+    for load, store in zip(loads, stores):
+        load.wait()
+        store.start()
+    for store in stores:
+        store.wait()
+
+
 def local(inputs, up_grads, momentum, selected):
     lefts, rights = constants()
-    vmem, hbm = pl.BlockSpec(memory_space=pltpu.VMEM), pl.BlockSpec(memory_space=pl.ANY)
+    hbm = pl.BlockSpec(memory_space=pl.ANY)
     sums = STREAMS * 2 * STREAM_ROWS
-    return pl.pallas_call(
+    new, upd = pl.pallas_call(
         kernel,
         out_shape=(
             jax.ShapeDtypeStruct((1, ROWS, COLS), F32),
             jax.ShapeDtypeStruct((ROWS, COLS), BF16),
         ),
-        in_specs=[hbm, hbm, hbm, vmem, vmem, vmem],
+        in_specs=[hbm] * 6,
         out_specs=(hbm, hbm),
         scratch_shapes=[
+            pltpu.VMEM((1, 4, 8, 32), jnp.int32),
+            pltpu.VMEM(lefts.shape, BF16),
+            pltpu.VMEM(rights.shape, BF16),
             pltpu.VMEM((RING, 2, TOK, ROWS), BF16),
             pltpu.VMEM((RING, 2, ROWS, TOK), BF16),
             pltpu.VMEM((RING, FIRST * SPAN, TOK), BF16),
@@ -342,26 +399,26 @@
             pltpu.VMEM((sums, COLS), BF16),
             pltpu.VMEM((SPAN, COLS), BF16),
             pltpu.VMEM((SPAN, COLS), BF16),
-            pltpu.VMEM((SPAN, COLS), F32),
-            pltpu.VMEM((ROWS, COLS), F32),
+                pltpu.VMEM((ROWS, COLS), F32),
             pltpu.VMEM((ROWS, COLS), F32),
             pltpu.VMEM((ROWS, COLS), F32),
             pltpu.VMEM((REPS, LISTS, 128), jnp.int32),
             pltpu.VMEM((REPS, LISTS, 128), F32),
             pltpu.VMEM((LISTS, SPAN, REPS * 128), BF16),
-            pltpu.VMEM((LISTS, HALF, REPS * 128), BF16),
+            pltpu.VMEM((LISTS, REPS * 128, HALF), BF16),
             pltpu.VMEM((LISTS, HALF, 128), BF16),
+            pltpu.VMEM((LISTS, SPAN, HALF), F32),
             pltpu.VMEM((ROWS, COLS), F32),
             pltpu.VMEM((ROWS, COLS), BF16),
-            pltpu.SemaphoreType.DMA((18,)),
+            pltpu.SemaphoreType.DMA((21,)),
             pltpu.SemaphoreType.DMA((10,)),
             pltpu.SemaphoreType.DMA((10,)),
             pltpu.SemaphoreType.DMA((1,)),
             pltpu.SemaphoreType.DMA((2, STREAMS, 4)),
-            pltpu.SemaphoreType.DMA((1,)),
-            pltpu.SemaphoreType.DMA((1,)),
-            pltpu.SemaphoreType.DMA((1,)),
-            pltpu.SemaphoreType.DMA((1,)),
+            pltpu.SemaphoreType.DMA((2,)),
+            pltpu.SemaphoreType.DMA((len(AROUND),)),
+            pltpu.SemaphoreType.DMA((2,)),
+            pltpu.SemaphoreType.DMA((len(AROUND),)),
             pltpu.SemaphoreType.DMA((2,)),
         ],
         compiler_params=pltpu.CompilerParams(
@@ -369,6 +426,18 @@
         ),
         cost_estimate=pl.CostEstimate(flops=4 * 10**9, bytes_accessed=8 * 10**6, transcendentals=0),
     )(inputs, up_grads, momentum, selected, jnp.asarray(lefts), jnp.asarray(rights))
+    return pl.pallas_call(
+        hand_on,
+        out_shape=(jax.ShapeDtypeStruct((1, ROWS, COLS), F32), jax.ShapeDtypeStruct((ROWS, COLS), BF16)),
+        in_specs=[hbm, hbm],
+        out_specs=(hbm, hbm),
+        scratch_shapes=[
+            pltpu.VMEM((ROWS, COLS), F32),
+            pltpu.VMEM((ROWS, COLS), BF16),
+            pltpu.SemaphoreType.DMA((8,)),
+            pltpu.SemaphoreType.DMA((8,)),
+        ],
+    )(new, upd)
 
 
 def solution(mesh):

time: 66.7 us -> 61.7 us (0.925)
  local copies, waits for them, and re-layouts: 3.54 us -> 0 us
  Pallas kernels: 62.3 us -> 60.9 us
    unnamed x2 -> x0, local copies, waits for them, and re-layouts: 3.54 us -> none
    pallas_call x1, Pallas kernels: 62.3 us -> 58.9 us  [local(): pl.pallas_call(kernel, out_shape=(jax.ShapeDtypeStruct((1, ROWS, COLS), F...]
    pallas_call x0 -> x1, Pallas kernels: none -> 1.97 us  [local(): pl.pallas_call(hand_on, out_shape=(jax.ShapeDtypeStruct((1, ROWS, COLS),...]
where the time goes in v2:
time: 61.7 us; the launch traced here: 61.5 us
  Pallas kernels  60.9 us (99%)
  between operations  0.64 us (1%)
    pallas_call x1, Pallas kernels, local(): pl.pallas_call(kernel, out_shape=(jax.ShapeDtypeStruct((1, ROWS, COLS), F...  58.9 us
    pallas_call x1, Pallas kernels, local(): pl.pallas_call(hand_on, out_shape=(jax.ShapeDtypeStruct((1, ROWS, COLS),...  1.97 us

profile of v2, /device:TPU:1, one launch (start us, length us, event | category | flops | bytes accessed | tf_op | source)
XLA Modules:
  0.0 61.5 jit_solution(5605820044454145482)
XLA Ops:
  0.6 58.9 %shard_map.77 = (f32[1,256,512]{2,1,0:T(8,128)}, bf16[256,512]{1,0:T(8,128)(2,1)}) custom-call(bf16[1,256,4096]{2,1,0:T(8,128)(2,1)} %x_hbm.1, bf16[1,256,512]{2,1,0:T(8,128)(2,1)} %g_hbm.1, f32[1,256,512]{2,1,0:T(8,128)} %m_hbm.1, s32[1,4,8,32]{3,2,1,0:T(8,128)} %sel_hbm.1, bf16[2,64,256]{2,1,0:T(8,128)(2,1)} %constant.4.clone.left_hbm, ...), custom_call_target="tpu_custom_call" | custom-call | flops 4000000000 | bytes 8000000 | tf_op jit(solution)/shard_map/pallas_call | solution.py:380
  59.6 2.0 %shard_map.78 = (f32[1,256,512]{2,1,0:T(8,128)}, bf16[256,512]{1,0:T(8,128)(2,1)}) custom-call(f32[1,256,512]{2,1,0:T(8,128)} %get-tuple-element.4.new_ref, bf16[256,512]{1,0:T(8,128)(2,1)} %get-tuple-element.5.upd_ref), custom_call_target="tpu_custom_call" | custom-call | tf_op jit(solution)/shard_map/pallas_call | solution.py:429

commit v3 on v2

--- a/solution.py
+++ b/solution.py
@@ -11,6 +11,7 @@
 SPAN, ROWS, COLS, TOK, RING, REPS = 64, 256, 512, 256, 8, 32
 HALF = COLS // 2
 AROUND = (0, 4, 3, 5, 2, 6, 1, 7)
+GROUP = 8
 LISTS = 8
 decay, epsilon = 0.999, 1e-06
 FIRST = 3
@@ -76,37 +77,42 @@
     z, x_hi = fsdp // 2, fsdp % 2
     partner = (rep, z * 2 + 1 - x_hi)
     ways = [(rep, ((z + 1) % RING) * 2 + x_hi), (rep, ((z + RING - 1) % RING) * 2 + x_hi)]
-    near = [
-        (((x_lo + dx) % 2) * 16 + y * 2 + (core + dc) % 2, fsdp) for dx in (0, 1) for dc in (0, 1) if dx + dc > 0
-    ]
-    far = {dy: (x_lo * 16 + ((y + dy) % 8) * 2 + core, fsdp) for dy in AROUND[1:]}
-
-    barrier = pltpu.get_barrier_semaphore()
-    for device in [partner, *ways, *near, *far.values()]:
-        pl.semaphore_signal(barrier, inc=1, device_id=device, device_id_type=MESH)
-
-    sel_load = pltpu.make_async_copy(sel_hbm, sel_ref, load_sem.at[18])
-    sel_load.start()
-    g_load = pltpu.make_async_copy(g_hbm.at[0], g_own, load_sem.at[0])
-    g_load.start()
+    def there(dy, dx, dc):
+        return (((x_lo + dx) % 2) * 16 + ((y + dy) % 8) * 2 + (core + dc) % 2, fsdp)
+
+    around = [(dy, dx, dc) for dy in AROUND for dx in (0, 1) for dc in (0, 1)]
+    near = [there(*d) for d in around[1:4]]
+    far = {dy: there(dy, 0, 0) for dy in AROUND[1:]}
+
     order = (4, 3, 5, 2, 6, 1, 7, 0)
     x_loads = {}
-    for n, dz in enumerate(order):
-        for kind in (1, 0):
-            column = ((z + dz) % RING) * 512 + (x_hi if kind == 0 else 1 - x_hi) * 256
-            cp = pltpu.make_async_copy(
-                x_hbm.at[0, :, pl.ds(pl.multiple_of(column, 256), 256)],
-                x_in.at[dz, kind],
-                load_sem.at[2 + 2 * n + kind],
-            )
-            cp.start()
-            x_loads[dz, kind] = cp
-    m_load = pltpu.make_async_copy(m_hbm.at[0], mom, load_sem.at[1])
-    m_load.start()
+
+    def load_x(dz, kind):
+        column = ((z + dz) % RING) * 512 + (x_hi if kind == 0 else 1 - x_hi) * 256
+        x_loads[dz, kind] = pltpu.make_async_copy(
+            x_hbm.at[0, :, pl.ds(pl.multiple_of(column, 256), 256)], x_in.at[dz, kind], load_sem.at[2 * dz + kind]
+        )
+        x_loads[dz, kind].start()
+
+    sel_load = pltpu.make_async_copy(sel_hbm, sel_ref, load_sem.at[16])
+    g_load = pltpu.make_async_copy(g_hbm.at[0], g_own, load_sem.at[17])
+    sel_load.start()
+    load_x(4, 1)
+    load_x(4, 0)
+    g_load.start()
+
+    barrier = pltpu.get_barrier_semaphore()
+    for device in [partner, *ways, *(there(*d) for d in around[1:])]:
+        pl.semaphore_signal(barrier, inc=1, device_id=device, device_id_type=MESH)
+
+    for dz in order[1:]:
+        load_x(dz, 1)
+        load_x(dz, 0)
+    m_load = pltpu.make_async_copy(m_hbm.at[0], mom, load_sem.at[18])
     left_load = pltpu.make_async_copy(left_hbm, left_ref, load_sem.at[19])
-    left_load.start()
     right_load = pltpu.make_async_copy(right_hbm, right_ref, load_sem.at[20])
-    right_load.start()
+    for cp in (m_load, left_load, right_load):
+        cp.start()
 
     sel_load.wait()
     rows = []
@@ -116,7 +122,7 @@
     own_ids = jnp.concatenate(rows, axis=0)
     ids[0] = own_ids
 
-    pl.semaphore_wait(barrier, 3 + len(near) + len(far))
+    pl.semaphore_wait(barrier, 3 + REPS - 1)
 
     def remote(src, dst, send_sem, recv_sem, device):
         cp = pltpu.make_async_remote_copy(
@@ -192,15 +198,15 @@
         by_column = (row & 63) + (lane >> 5) * SPAN == count_n
         return by_row.astype(F32).astype(BF16), by_column.astype(F32).astype(BF16)
 
-    def send_near(slots, send_sem, recv_sem):
+    def send_near():
         for n, device in enumerate(near):
-            remote(slots.at[0], slots.at[1 + n], send_sem.at[0], recv_sem.at[0], device)
-
-    def send_far(slots, send_sem, recv_sem):
-        landed(slots, recv_sem, 0)
+            remote(ids.at[0], ids.at[1 + n], is_sem.at[0], ir_sem.at[0], device)
+
+    def send_far():
+        landed(0)
         for dy, device in far.items():
             n = AROUND.index(8 - dy)
-            remote(slots.at[pl.ds(0, 4)], slots.at[pl.ds(4 * n, 4)], send_sem.at[1], recv_sem.at[n], device)
+            remote(ids.at[pl.ds(0, 4)], ids.at[pl.ds(4 * n, 4)], is_sem.at[1], ir_sem.at[n], device)
 
     def of_size(slots, count, send_sem, recv_sem):
         at = slots.at[pl.ds(0, count)]
@@ -208,12 +214,8 @@
             src_ref=at, dst_ref=at, send_sem=send_sem, recv_sem=recv_sem, device_id=partner, device_id_type=MESH
         )
 
-    def landed(slots, recv_sem, n):
-        of_size(slots, 3 if n == 0 else 4, is_sem.at[0], recv_sem.at[n]).wait_recv()
-
-    def sent(slots, send_sem):
-        of_size(slots, 3, send_sem.at[0], ir_sem.at[0]).wait_send()
-        of_size(slots, 28, send_sem.at[1], ir_sem.at[0]).wait_send()
+    def landed(n):
+        of_size(ids, 3 if n == 0 else 4, is_sem.at[0], ir_sem.at[n]).wait_recv()
 
     def build(first, count):
         def one(r, carry):
@@ -249,14 +251,14 @@
             kept.append(jnp.sum(jnp.where(by_row, both[:SPAN] + both[SPAN:], 0.0), axis=0, keepdims=True))
         vals[0, pl.ds(2 * a, 2)] = jnp.concatenate(kept, axis=0)
 
-    send_near(ids, is_sem, ir_sem)
+    send_near()
     g_send = remote(g_hbm.at[0], g_got, xs_sem.at[8], xr_sem.at[8], partner)
     turn(4)
     g_load.wait()
     chain(3, 0)
     chain(4, 0)
     turn(3, 5)
-    send_far(ids, is_sem, ir_sem)
+    send_far()
     chain(3, 1)
     chain(4, 1)
     turn(2, 6)
@@ -276,7 +278,7 @@
     wait_x(5)
     chain(0, 1)
     for n in range(1, 8):
-        landed(ids, ir_sem, n)
+        landed(n)
     build(4, 3)
     chain(1, 1)
     build(7, 3)
@@ -307,10 +309,10 @@
         grad[pl.ds(s * SPAN, SPAN), :] = finish(s)
         transform(s)
 
-    send_near(vals, vs_sem, vr_sem)
+    for dy, dx, dc in around[1:]:
+        slot = around.index(((8 - dy) % 8, dx, dc))
+        remote(vals.at[0], vals.at[slot], vs_sem.at[0], vr_sem.at[slot // GROUP], there(dy, dx, dc))
     for a in range(4):
-        if a == 2:
-            send_far(vals, vs_sem, vr_sem)
         at = pl.ds(a * SPAN, SPAN)
         partly = from_left(left_ref[1], coef[at, :] * mask[at, :])
         for h in range(2):
@@ -320,19 +322,16 @@
     new_store = pltpu.make_async_copy(new_v, new_hbm.at[0], out_sem.at[0])
     new_store.start()
 
-    for first, last in ((0, 1), (1, 4), (4, 6), (6, 8)):
-        for n in range(max(first, 1), last):
-            landed(vals, vr_sem, n)
+    for group in range(REPS // GROUP):
+        of_size(vals, GROUP - (group == 0), vs_sem.at[0], vr_sem.at[group]).wait_recv()
+        first, last = group * GROUP, (group + 1) * GROUP
         for s in range(LISTS):
             weighted = jnp.concatenate(
-                [
-                    l_hot[s, :, r * 128 : (r + 1) * 128] * vals[r, s : s + 1, :].astype(BF16)
-                    for r in range(4 * first, 4 * last)
-                ],
+                [l_hot[s, :, r * 128 : (r + 1) * 128] * vals[r, s : s + 1, :].astype(BF16) for r in range(first, last)],
                 axis=1,
             )
-            term = dot(weighted, r_hot[s, pl.ds(4 * first * 128, 4 * (last - first) * 128)])
-            total[s] = term if first == 0 else total[s] + term
+            term = dot(weighted, r_hot[s, pl.ds(first * 128, GROUP * 128)])
+            total[s] = term if group == 0 else total[s] + term
     power = jnp.concatenate([jnp.sum(total[s] * total[s], axis=0, keepdims=True) for s in range(LISTS)], axis=0)
     hi, lo = split(power)
     power = dot(hi, right_ref[4]) + dot(lo, right_ref[4])
@@ -352,8 +351,9 @@
         src_ref=sums_out, dst_ref=sums_out, send_sem=zs_sem.at[0], recv_sem=zr_sem.at[0, 0, 0],
         device_id=partner, device_id_type=MESH,
     ).wait_send()
-    sent(ids, is_sem)
-    sent(vals, vs_sem)
+    of_size(ids, 3, is_sem.at[0], ir_sem.at[0]).wait_send()
+    of_size(ids, 28, is_sem.at[1], ir_sem.at[0]).wait_send()
+    of_size(vals, REPS - 1, vs_sem.at[0], vr_sem.at[0]).wait_send()
     new_store.wait()
     upd_store.wait()
 
@@ -417,8 +417,8 @@
             pltpu.SemaphoreType.DMA((2, STREAMS, 4)),
             pltpu.SemaphoreType.DMA((2,)),
             pltpu.SemaphoreType.DMA((len(AROUND),)),
-            pltpu.SemaphoreType.DMA((2,)),
-            pltpu.SemaphoreType.DMA((len(AROUND),)),
+            pltpu.SemaphoreType.DMA((1,)),
+            pltpu.SemaphoreType.DMA((REPS // GROUP,)),
             pltpu.SemaphoreType.DMA((2,)),
         ],
         compiler_params=pltpu.CompilerParams(

time: 61.7 us -> 60.5 us (0.981)
  Pallas kernels: 60.9 us -> 59.7 us
    pallas_call x1, Pallas kernels: 58.9 us -> 57.7 us  [local(): pl.pallas_call(kernel, out_shape=(jax.ShapeDtypeStruct((1, ROWS, COLS), F...]
where the time goes in v3:
time: 60.5 us; the launch traced here: 60.3 us
  Pallas kernels  59.7 us (99%)
  between operations  0.64 us (1%)
    pallas_call x1, Pallas kernels, local(): pl.pallas_call(kernel, out_shape=(jax.ShapeDtypeStruct((1, ROWS, COLS), F...  57.7 us
    pallas_call x1, Pallas kernels, local(): pl.pallas_call(hand_on, out_shape=(jax.ShapeDtypeStruct((1, ROWS, COLS),...  1.97 us

profile of v3, /device:TPU:1, one launch (start us, length us, event | category | flops | bytes accessed | tf_op | source)
XLA Modules:
  0.0 60.3 jit_solution(10706508591823461825)
XLA Ops:
  0.6 57.7 %shard_map.77 = (f32[1,256,512]{2,1,0:T(8,128)}, bf16[256,512]{1,0:T(8,128)(2,1)}) custom-call(bf16[1,256,4096]{2,1,0:T(8,128)(2,1)} %x_hbm.1, bf16[1,256,512]{2,1,0:T(8,128)(2,1)} %g_hbm.1, f32[1,256,512]{2,1,0:T(8,128)} %m_hbm.1, s32[1,4,8,32]{3,2,1,0:T(8,128)} %sel_hbm.1, bf16[2,64,256]{2,1,0:T(8,128)(2,1)} %constant.4.clone.left_hbm, ...), custom_call_target="tpu_custom_call" | custom-call | flops 4000000000 | bytes 8000000 | tf_op jit(solution)/shard_map/pallas_call | solution.py:380
  58.3 2.0 %shard_map.78 = (f32[1,256,512]{2,1,0:T(8,128)}, bf16[256,512]{1,0:T(8,128)(2,1)}) custom-call(f32[1,256,512]{2,1,0:T(8,128)} %get-tuple-element.4.new_ref, bf16[256,512]{1,0:T(8,128)(2,1)} %get-tuple-element.5.upd_ref), custom_call_target="tpu_custom_call" | custom-call | tf_op jit(solution)/shard_map/pallas_call | solution.py:429

commit v4 on v3

--- a/solution.py
+++ b/solution.py
@@ -173,8 +173,9 @@
                 sums_out[pl.ds(offset(way, stream, 0), 32), :] = term[32 * way : 32 * way + 32]
                 send_sum(way, stream, 0)
             return
+        terms = [product(stream, 4 - step), product(stream, 4 + step)]
         for way in range(2):
-            term = product(stream, 4 - step if way == 0 else 4 + step)
+            term = terms[way]
             got = arrived(way, stream, step - 1)
             at = offset(way, stream, step)
             if step == 1:

time: 60.5 us -> 60.5 us (level)
  no operation moved by 1% of the time
where the time goes in v4:
time: 60.5 us; the launch traced here: 60.3 us
  Pallas kernels  59.7 us (99%)
  between operations  0.64 us (1%)
    pallas_call x1, Pallas kernels, local(): pl.pallas_call(kernel, out_shape=(jax.ShapeDtypeStruct((1, ROWS, COLS), F...  57.7 us
    pallas_call x1, Pallas kernels, local(): pl.pallas_call(hand_on, out_shape=(jax.ShapeDtypeStruct((1, ROWS, COLS),...  1.97 us

profile of v4, /device:TPU:1, one launch (start us, length us, event | category | flops | bytes accessed | tf_op | source)
XLA Modules:
  0.0 60.3 jit_solution(12551595449819024840)
XLA Ops:
  0.6 57.7 %shard_map.77 = (f32[1,256,512]{2,1,0:T(8,128)}, bf16[256,512]{1,0:T(8,128)(2,1)}) custom-call(bf16[1,256,4096]{2,1,0:T(8,128)(2,1)} %x_hbm.1, bf16[1,256,512]{2,1,0:T(8,128)(2,1)} %g_hbm.1, f32[1,256,512]{2,1,0:T(8,128)} %m_hbm.1, s32[1,4,8,32]{3,2,1,0:T(8,128)} %sel_hbm.1, bf16[2,64,256]{2,1,0:T(8,128)(2,1)} %constant.4.clone.left_hbm, ...), custom_call_target="tpu_custom_call" | custom-call | flops 4000000000 | bytes 8000000 | tf_op jit(solution)/shard_map/pallas_call | solution.py:381
  58.3 2.0 %shard_map.78 = (f32[1,256,512]{2,1,0:T(8,128)}, bf16[256,512]{1,0:T(8,128)(2,1)}) custom-call(f32[1,256,512]{2,1,0:T(8,128)} %get-tuple-element.4.new_ref, bf16[256,512]{1,0:T(8,128)(2,1)} %get-tuple-element.5.upd_ref), custom_call_target="tpu_custom_call" | custom-call | tf_op jit(solution)/shard_map/pallas_call | solution.py:430
